TPU v7x, 128 devices: a whole 4x4x4 slice. The times are simulated.
128 devices in a mesh: row: 16 (over y, x), col: 8 (over z, core).
Axes of the slice: x: 4, y: 4, z: 4, core: 2. Of those that a mesh axis runs over, the one named last changes fastest.
Arguments:
- out_grad: bfloat16 [131072, 256], P(('row', 'col')), may hold values from -6 to 6
- features: bfloat16 [131072, 256], P(('col', 'row')), may hold values from -6 to 6
- weight: bfloat16 [256, 256], replicated, may hold values from -0.375 to 0.375
- tiles: bfloat16 [16, 8, 384, 128, 128], P('row', 'col'), may hold values from -0.07470703 to 0.07470703
- row_block: int32 [16, 8, 384], P('row', 'col'), may hold values from 0 to 63
- col_block: int32 [16, 8, 384], P('row', 'col'), may hold values from 0 to 127
- live: int32 [16, 8, 384], P('row', 'col'), may hold values from 0 to 1, as said below
Outputs:
- input_grad: bfloat16 [131072, 256], P(('col', 'row'))
- weight_grad: float32 [256, 256], replicated
Inputs may be any that keep to these rules, and one draw needn't show every extreme that they name: Each cell's slots of live hold between 48 and 384 ones, and in some cell all 384 slots are live.
All inputs are finite; a program needn't handle non-finite values.
Results may differ from a plain program's by a relative error of at most 0.0049.
Values may be sent and summed in bfloat16 or wider, within the bound.
No kernel may reach another device: no remote copies, remote signals or barrier semaphores. Data moves between devices by JAX's collectives and lax.ppermute only.
A program may use at most 256 MiB of HBM per device.

v0:
```python
import jax
import jax.numpy as jnp
from jax import lax
from jax.sharding import PartitionSpec as P


def local(out_grad, features, weight, tiles, row_block, col_block, live):
    tile_set = tiles[0, 0]
    row_ids = row_block[0, 0]
    col_ids = col_block[0, 0]
    live_weights = live[0, 0].astype(jnp.float32)
    tile_size = tile_set.shape[-1]
    feature_width = out_grad.shape[1]
    own_rows = features.shape[0]
    group_rows = lax.all_gather(out_grad, "col", axis=0, tiled=True)
    grad_blocks = group_rows.reshape(-1, tile_size, feature_width)
    column_count = lax.axis_size("row") * own_rows // tile_size
    panels = grad_blocks[row_ids]
    contrib = jnp.einsum("kij,kif->kjf", tile_set, panels, preferred_element_type=jnp.float32)
    contrib = contrib * live_weights[:, None, None]
    partial_value = jax.ops.segment_sum(contrib, col_ids, num_segments=column_count)
    partial_value = partial_value.reshape(column_count * tile_size, feature_width)
    summed = lax.psum_scatter(partial_value, "row", scatter_dimension=0, tiled=True)
    column_grad = summed.astype(jnp.bfloat16)
    input_grad = jnp.einsum(
        "nf,gf->ng", column_grad, weight, preferred_element_type=jnp.float32
    ).astype(jnp.bfloat16)
    local_weight = jnp.einsum(
        "nf,ng->fg", features, column_grad, preferred_element_type=jnp.float32
    )
    summed_weight = lax.psum(local_weight, ("row", "col"))
    node_count = own_rows * lax.axis_size("row") * lax.axis_size("col")
    weight_grad = summed_weight * node_count ** (-0.5)
    return (input_grad, weight_grad)


def solution(mesh):
    return jax.shard_map(
        local,
        mesh=mesh,
        in_specs=(
            P(("row", "col"), None),
            P(("col", "row"), None),
            P(),
            P("row", "col", None, None, None),
            P("row", "col", None),
            P("row", "col", None),
            P("row", "col", None),
        ),
        out_specs=(P(("col", "row"), None), P()),
        check_vma=False,
    )
```

profile of v0, /device:TPU:1, one launch (start us, length us, event | category | flops | bytes accessed | tf_op | source)
XLA Modules:
  0.0 529.0 jit_solution(17368533770410654152)
XLA Ops:
  7.2 0.0 copy-start
  7.2 0.0 all-gather.2.cloned.1.call-start
  7.2 0.7 all-gather.2.cloned.1.call-update
  7.9 0.0 reduce-scatter.2.cloned.1.call-start
  8.0 0.7 reduce
  8.7 0.7 fusion.3
  9.4 0.7 convert_reduce_fusion
  10.1 35.7 %all-gather.2.cloned.1.call-done = bf16[8192,256]{1,0:T(8,128)(2,1)} async-done(((bf16[1024,256]{1,0:T(8,128)(2,1)}), bf16[8192,256]{1,0:T(8,128)(2,1)}) %all-gather.2.cloned.1.call-update) | async-done | bytes 4194320 | tf_op jit(solution)/shard_map/all_gather | solution.py:15
  45.7 15.1 %gather_fusion = bf16[384,128,256]{2,1,0:T(8,128)(2,1)} fusion(bf16[64,128,256]{2,1,0:T(8,128)(2,1)} %bitcast.15, s32[1024]{0:T(1024)S(1)} %pad_clamp_fusion), kind=kCustom, calls=%fused_computation | custom fusion | bytes 50333184 | tf_op jit(solution)/shard_map/gather | solution.py:18
  60.9 31.7 %multiply_bitcast_fusion = f32[384,128,256]{1,2,0:T(8,128)} fusion(f32[384]{0:T(512)S(1)} %convert_reduce_fusion, bf16[384,128,256]{2,1,0:T(8,128)(2,1)} %gather_fusion, bf16[1,1,384,128,128]{4,3,2,1,0:T(8,128)(2,1)} %param.10), kind=kOutput, calls=%fused_computation.2 | convolution fusion | flops 3233808384 | bytes 88081920 | tf_op jit(solution)/shard_map/kij,kif->kjf/dot_general | solution.py:19
  92.6 48.8 %copy.12 = f32[384,128,256]{2,1,0:T(8,128)} copy(f32[384,128,256]{1,2,0:T(8,128)} %multiply_bitcast_fusion) | data formatting | bytes 100663296 | tf_op jit(solution)/shard_map/mul | solution.py:20
  141.4 7.8 %broadcast_in_dim.2 = f32[128,128,256]{2,1,0:T(8,128)} broadcast(f32[]{:T(128)} %constant.0.clone.1), dimensions={} | broadcast | bytes 16777220 | tf_op jit(solution)/shard_map/broadcast_in_dim | solution.py:21
  149.2 0.0 copy-start.1
  149.2 114.9 %scatter_fusion = f32[128,128,256]{2,1,0:T(8,128)} fusion(f32[128,128,256]{2,1,0:T(8,128)} %broadcast_in_dim.2, s32[384]{0:T(512)S(1)} %reduce, f32[384,128,256]{2,1,0:T(8,128)} %copy.12), kind=kCustom, calls=%fused_computation.1 | custom fusion | flops 12582912 | bytes 150996480 | tf_op jit(solution)/shard_map/scatter-add | solution.py:21
  264.1 0.0 reduce-scatter.2.cloned.1.call-update
  264.1 0.0 all-reduce.2.cloned.1.call-start
  264.1 109.6 %reduce-scatter.2.cloned.1.call-done = f32[1024,256]{1,0:T(8,128)} async-done(((f32[16384,256]{1,0:T(8,128)}), f32[1024,256]{1,0:T(8,128)}) %reduce-scatter.2.cloned.1.call-update) | async-done | bytes 1048592 | tf_op jit(solution)/shard_map/reduce_scatter | solution.py:23
  373.7 0.0 copy-done
  373.8 2.3 convolution_bitcast_fusion
  376.0 0.0 all-reduce.2.cloned.1.call-update
  376.0 0.0 copy-done.1
  376.1 2.4 convolution_convert_fusion
  378.4 142.3 %all-reduce.2.cloned.1.call-done = f32[256,256]{0,1:T(8,128)} async-done(((f32[256,256]{0,1:T(8,128)}), f32[256,256]{0,1:T(8,128)}) %all-reduce.2.cloned.1.call-update) | async-done | bytes 262160 | tf_op jit(solution)/shard_map/psum | solution.py:31
  520.7 1.0 broadcast_multiply_fusion
  521.7 0.8 copy.13
  (1 shorter events, 0.0 us)
Async XLA Ops:
  7.2 366.6 %copy-start = (bf16[1024,256]{1,0:T(8,128)(2,1)S(1)}, bf16[1024,256]{1,0:T(8,128)(2,1)}, u32[]{:S(2)}) copy-start(bf16[1024,256]{1,0:T(8,128)(2,1)} %param.8) | copy-start | bytes 1572868
  7.2 38.5 %all-gather.2.cloned.1.call-start = ((), (), s32[]{:S(2)}) async-start(), calls=%async_computation.1 | async-start | bytes 4718592 | tf_op jit(solution)/shard_map/all_gather | solution.py:15
  7.9 365.8 %reduce-scatter.2.cloned.1.call-start = ((), (), s32[]{:S(2)}) async-start(), calls=%async_computation.2 | async-start | bytes 17825792 | tf_op jit(solution)/shard_map/reduce_scatter | solution.py:23
  149.2 226.9 %copy-start.1 = (bf16[256,256]{1,0:T(8,128)(2,1)S(1)}, bf16[256,256]{1,0:T(8,128)(2,1)}, u32[]{:S(2)}) copy-start(bf16[256,256]{1,0:T(8,128)(2,1)} %param.9) | copy-start | bytes 393220
  264.1 256.6 %all-reduce.2.cloned.1.call-start = ((), (), s32[]{:S(2)}) async-start(), calls=%async_computation.3 | async-start | bytes 524288 | tf_op jit(solution)/shard_map/psum | solution.py:31
Sparse Core Ops, SparseCore 0:
  9.7 35.9 all-gather.1
  264.2 109.5 reduce-scatter.1
  379.1 141.5 all-reduce.1
where the time goes:
time: 530 us; the launch traced here: 529 us
  waiting for transfers between devices  288 us (54%)
  other arithmetic  118 us (22%)
  local copies, waits for them, and re-layouts  72.6 us (14%)
  matrix products  36.3 us (7%)
  between operations  13.8 us (3%)
    psum x1, waiting for transfers between devices, local(): summed_weight = lax.psum(local_weight, ('row', 'col'))  142 us
    scatter-add x1, other arithmetic, local(): jax.ops.segment_sum(contrib, col_ids, num_segments=column_count)  115 us
    reduce_scatter x1, waiting for transfers between devices, local(): lax.psum_scatter(partial_value, 'row', scatter_dimension=0, tiled=True)  110 us
    mul x1, local copies, waits for them, and re-layouts, local(): contrib = contrib * live_weights[:, None, None]  48.8 us
    all_gather x1, waiting for transfers between devices, local(): group_rows = lax.all_gather(out_grad, 'col', axis=0, tiled=True)  35.7 us
    dot_general x1, matrix products, local(): jnp.einsum('kij,kif->kjf', tile_set, panels, preferred_element_type=jnp.f...  31.7 us
    gather x1, local copies, waits for them, and re-layouts, local(): panels = grad_blocks[row_ids]  15.1 us
  transfers between devices with their start and end apart: 3, of which 3 were waited for; matrix products, arithmetic and copies ran while one was open for 1% of the time, Pallas kernels for 0%

commit v1 on v0

--- a/solution.py
+++ b/solution.py
@@ -12,7 +12,10 @@
     tile_size = tile_set.shape[-1]
     feature_width = out_grad.shape[1]
     own_rows = features.shape[0]
-    group_rows = lax.all_gather(out_grad, "col", axis=0, tiled=True)
+    size = lax.axis_size("col")
+    blocks = jnp.stack([out_grad for _ in range(size)])
+    blocks = lax.all_to_all(blocks, "col", split_axis=0, concat_axis=0)
+    group_rows = jnp.concatenate(blocks, axis=0)
     grad_blocks = group_rows.reshape(-1, tile_size, feature_width)
     column_count = lax.axis_size("row") * own_rows // tile_size
     panels = grad_blocks[row_ids]

time: 530 us -> 552 us (1.042)
  waiting for transfers between devices: 288 us -> 299 us
  starting transfers between devices: 0.12 us -> 6.86 us
    all_to_all x0 -> x1, waiting for transfers between devices: none -> 46.8 us  [local(): blocks = lax.all_to_all(blocks, 'col', split_axis=0, concat_axis=0)]
    all_gather x1 -> x0, waiting for transfers between devices: 35.7 us -> none  [local(): group_rows = lax.all_gather(out_grad, 'col', axis=0, tiled=True)]
    all_to_all x0 -> x1, starting transfers between devices: none -> 6.81 us  [local(): blocks = lax.all_to_all(blocks, 'col', split_axis=0, concat_axis=0)]
where the time goes in v1:
time: 552 us; the launch traced here: 551 us
  waiting for transfers between devices  299 us (54%)
  other arithmetic  118 us (21%)
  local copies, waits for them, and re-layouts  75.9 us (14%)
  matrix products  36.4 us (7%)
  between operations  14.1 us (3%)
  starting transfers between devices  6.86 us (1%)
    psum x1, waiting for transfers between devices, local(): summed_weight = lax.psum(local_weight, ('row', 'col'))  142 us
    scatter-add x1, other arithmetic, local(): jax.ops.segment_sum(contrib, col_ids, num_segments=column_count)  115 us
    reduce_scatter x1, waiting for transfers between devices, local(): lax.psum_scatter(partial_value, 'row', scatter_dimension=0, tiled=True)  110 us
    mul x1, local copies, waits for them, and re-layouts, local(): contrib = contrib * live_weights[:, None, None]  48.8 us
    all_to_all x1, waiting for transfers between devices, local(): blocks = lax.all_to_all(blocks, 'col', split_axis=0, concat_axis=0)  46.8 us
    dot_general x1, matrix products, local(): jnp.einsum('kij,kif->kjf', tile_set, panels, preferred_element_type=jnp.f...  31.7 us
    gather x1, local copies, waits for them, and re-layouts, local(): panels = grad_blocks[row_ids]  15.1 us
  transfers between devices with their start and end apart: 3, of which 3 were waited for; matrix products, arithmetic and copies ran while one was open for 1% of the time, Pallas kernels for 0%

profile of v1, /device:TPU:1, one launch (start us, length us, event | category | flops | bytes accessed | tf_op | source)
XLA Modules:
  0.0 550.5 jit_solution(7422897808771373747)
XLA Ops:
  7.2 0.0 copy-start
  7.2 3.3 stack.2
  10.5 6.8 %all-to-all-start = ((bf16[8,1024,256]{2,1,0:T(8,128)(2,1)}), bf16[8,1024,256]{2,1,0:T(8,128)(2,1)}, u32[]{:S(2)}, u32[]{:S(2)}) async-start(bf16[8,1024,256]{2,1,0:T(8,128)(2,1)} %stack.2), calls=%async_computation | async-start | bytes 8388608 | tf_op jit(solution)/shard_map/all_to_all | solution.py:17
  17.3 0.0 reduce-scatter.2.cloned.1.call-start
  17.3 0.7 reduce
  18.0 0.7 fusion.3
  18.7 0.7 convert_reduce_fusion
  19.4 46.8 %all-to-all-done = bf16[8,1024,256]{2,1,0:T(8,128)(2,1)} async-done(((bf16[8,1024,256]{2,1,0:T(8,128)(2,1)}), bf16[8,1024,256]{2,1,0:T(8,128)(2,1)}, u32[]{:S(2)}, u32[]{:S(2)}) %all-to-all-start) | async-done | bytes 4194336 | tf_op jit(solution)/shard_map/all_to_all | solution.py:17
  66.2 15.1 %gather_fusion = bf16[384,128,256]{2,1,0:T(8,128)(2,1)} fusion(bf16[64,128,256]{2,1,0:T(8,128)(2,1)} %bitcast, s32[1024]{0:T(1024)S(1)} %pad_clamp_fusion), kind=kCustom, calls=%fused_computation | custom fusion | bytes 50333184 | tf_op jit(solution)/shard_map/gather | solution.py:21
  81.3 31.7 %multiply_bitcast_fusion = f32[384,128,256]{1,2,0:T(8,128)} fusion(f32[384]{0:T(512)S(1)} %convert_reduce_fusion, bf16[384,128,256]{2,1,0:T(8,128)(2,1)} %gather_fusion, bf16[1,1,384,128,128]{4,3,2,1,0:T(8,128)(2,1)} %param.10), kind=kOutput, calls=%fused_computation.2 | convolution fusion | flops 3233808384 | bytes 88081920 | tf_op jit(solution)/shard_map/kij,kif->kjf/dot_general | solution.py:22
  113.1 48.8 %copy.12 = f32[384,128,256]{2,1,0:T(8,128)} copy(f32[384,128,256]{1,2,0:T(8,128)} %multiply_bitcast_fusion) | data formatting | bytes 100663296 | tf_op jit(solution)/shard_map/mul | solution.py:23
  161.9 7.8 %broadcast_in_dim.2 = f32[128,128,256]{2,1,0:T(8,128)} broadcast(f32[]{:T(128)} %constant.0.clone.1), dimensions={} | broadcast | bytes 16777220 | tf_op jit(solution)/shard_map/broadcast_in_dim | solution.py:24
  169.7 0.0 copy-start.1
  169.7 114.9 %scatter_fusion = f32[128,128,256]{2,1,0:T(8,128)} fusion(f32[128,128,256]{2,1,0:T(8,128)} %broadcast_in_dim.2, s32[384]{0:T(512)S(1)} %reduce, f32[384,128,256]{2,1,0:T(8,128)} %copy.12), kind=kCustom, calls=%fused_computation.1 | custom fusion | flops 12582912 | bytes 150996480 | tf_op jit(solution)/shard_map/scatter-add | solution.py:24
  284.5 0.0 reduce-scatter.2.cloned.1.call-update
  284.6 0.0 all-reduce.2.cloned.1.call-start
  284.6 110.3 %reduce-scatter.2.cloned.1.call-done = f32[1024,256]{1,0:T(8,128)} async-done(((f32[16384,256]{1,0:T(8,128)}), f32[1024,256]{1,0:T(8,128)}) %reduce-scatter.2.cloned.1.call-update) | async-done | bytes 1048592 | tf_op jit(solution)/shard_map/reduce_scatter | solution.py:26
  394.9 0.0 copy-done
  394.9 2.3 convolution_bitcast_fusion
  397.2 0.0 all-reduce.2.cloned.1.call-update
  397.2 0.0 copy-done.1
  397.2 2.4 convolution_convert_fusion
  399.6 142.3 %all-reduce.2.cloned.1.call-done = f32[256,256]{0,1:T(8,128)} async-done(((f32[256,256]{0,1:T(8,128)}), f32[256,256]{0,1:T(8,128)}) %all-reduce.2.cloned.1.call-update) | async-done | bytes 262160 | tf_op jit(solution)/shard_map/psum | solution.py:34
  541.9 1.0 broadcast_multiply_fusion
  542.8 0.8 copy.13
  (1 shorter events, 0.0 us)
Async XLA Ops:
  7.2 387.7 %copy-start = (bf16[1024,256]{1,0:T(8,128)(2,1)S(1)}, bf16[1024,256]{1,0:T(8,128)(2,1)}, u32[]{:S(2)}) copy-start(bf16[1024,256]{1,0:T(8,128)(2,1)} %param.8) | copy-start | bytes 1572868
  10.5 55.7 %all-to-all-start = ((bf16[8,1024,256]{2,1,0:T(8,128)(2,1)}), bf16[8,1024,256]{2,1,0:T(8,128)(2,1)}, u32[]{:S(2)}, u32[]{:S(2)}) async-start(bf16[8,1024,256]{2,1,0:T(8,128)(2,1)} %stack.2), calls=%async_computation | async-start | bytes 8388608 | tf_op jit(solution)/shard_map/all_to_all | solution.py:17
  17.3 377.6 %reduce-scatter.2.cloned.1.call-start = ((), (), s32[]{:S(2)}) async-start(), calls=%async_computation.2 | async-start | bytes 17825792 | tf_op jit(solution)/shard_map/reduce_scatter | solution.py:26
  169.7 227.5 %copy-start.1 = (bf16[256,256]{1,0:T(8,128)(2,1)S(1)}, bf16[256,256]{1,0:T(8,128)(2,1)}, u32[]{:S(2)}) copy-start(bf16[256,256]{1,0:T(8,128)(2,1)} %param.9) | copy-start | bytes 393220
  284.6 257.3 %all-reduce.2.cloned.1.call-start = ((), (), s32[]{:S(2)}) async-start(), calls=%async_computation.3 | async-start | bytes 524288 | tf_op jit(solution)/shard_map/psum | solution.py:34
Sparse Core Ops, SparseCore 0:
  284.7 110.1 reduce-scatter.1
  400.2 141.6 all-reduce.1
